TPU v7x, 128 devices: a whole 4x4x4 slice. The times are simulated.
128 devices in a mesh: section: 2 (over core), seq: 8 (over y, x_lo), mp: 8 (over x_hi, z).
Axes of the slice: x: 4 (x_hi: 2, x_lo: 2; x = x_hi * 2 + x_lo), y: 4, z: 4, core: 2. Of those that a mesh axis runs over, the one named last changes fastest.
Arguments:
- bottleneck: bfloat16 [2, 1024, 4096], P('section', ('seq', 'mp')), may hold values from -6 to 6
- qkv_weight: bfloat16 [3, 4096, 4096], P(None, None, ('section', 'mp')), may hold values from -0.2 to 0.2
- out_weight: bfloat16 [4096, 4096], P(('section', 'mp')), may hold values from -0.5 to 0.5
- up_weight: bfloat16 [4096, 16384], P(None, ('section', 'mp')), may hold values from -0.09375 to 0.09375
- down_weight: bfloat16 [16384, 4096], P(('section', 'mp')), may hold values from -0.046875 to 0.046875
- cotangent: bfloat16 [2, 1024, 4096], P('section', ('seq', 'mp')), may hold values from -6 to 6
Outputs:
- block_out: bfloat16 [2, 1024, 4096], P('section', ('seq', 'mp'))
- grad_input: bfloat16 [2, 1024, 4096], P('section', ('seq', 'mp'))
All inputs are finite; a program needn't handle non-finite values.
Results may differ from a plain program's by a relative error of at most 0.025.
Values may be sent and summed in bfloat16 or wider, within the bound.
No kernel may reach another device: no remote copies, remote signals or barrier semaphores. Data moves between devices by JAX's collectives and lax.ppermute only.
A program may use at most 128 MiB of HBM per device.

v0:
```python
import math
import jax
import jax.numpy as jnp
from jax import lax
from jax.sharding import PartitionSpec as P

HD = 128
norm_eps = 1e-06


def layer_norm(inputs):
    row_mean = jnp.mean(inputs, axis=-1, keepdims=True)
    centered = inputs - row_mean
    inv_std = lax.rsqrt(jnp.mean(centered * centered, axis=-1, keepdims=True) + norm_eps)
    return (centered * inv_std, inv_std)


def norm_backward(normed, inv_std, grad_in):
    mean_grad = jnp.mean(grad_in, axis=-1, keepdims=True)
    mean_mix = jnp.mean(grad_in * normed, axis=-1, keepdims=True)
    return inv_std * (grad_in - mean_grad - normed * mean_mix)


def gelu_value(pre_act):
    return pre_act * 0.5 * (1.0 + lax.erf(pre_act * 0.7071067811865476))


def gelu_slope(pre_act):
    cumul = 0.5 * (1.0 + lax.erf(pre_act * 0.7071067811865476))
    return cumul + pre_act * jnp.exp(-0.5 * pre_act * pre_act) * 0.3989422804014327


def swap_section(data):
    return lax.ppermute(data, "section", [(0, 1), (1, 0)])


def spread(own, axis):
    size = lax.axis_size(axis)
    copies = jnp.broadcast_to(own[None], (size,) + own.shape)
    return lax.all_to_all(copies, axis, 0, 0)


def gather_rows(own):
    mine = spread(own, "mp").reshape(-1, own.shape[-1])
    return jnp.concatenate([mine, swap_section(mine)], axis=0)


def scatter_rows(partial):
    half = partial.shape[0] // 2
    width = partial.shape[1]
    other = swap_section(partial[half:].astype(jnp.bfloat16))
    pair = (partial[:half] + other.astype(jnp.float32)).astype(jnp.bfloat16)
    size = lax.axis_size("mp")
    parts = lax.all_to_all(pair.reshape(size, half // size, width), "mp", 0, 0)
    return jnp.sum(parts.astype(jnp.float32), axis=0)


def scatter_rows_later(partial):
    half = partial.shape[0] // 2
    other = swap_section(partial[half:].astype(jnp.bfloat16))
    pair = (partial[:half] + other.astype(jnp.float32)).astype(jnp.bfloat16)
    return lax.psum_scatter(pair, "mp", scatter_dimension=0, tiled=True).astype(jnp.float32)


def gather_rows_early(own):
    mine = lax.all_gather(own, "mp", axis=0, tiled=True)
    return jnp.concatenate([mine, swap_section(mine)], axis=0)


def dot_f32(lhs, rhs):
    return jnp.dot(lhs, rhs, preferred_element_type=jnp.float32)


def dot_nt(lhs, rhs):
    return jnp.einsum("tf,df->td", lhs, rhs, preferred_element_type=jnp.float32)


def per_device(bottleneck, qkv_weight, out_weight, up_weight, down_weight, cotangent):
    own_in = bottleneck[0].astype(jnp.float32)
    own_cot = cotangent[0]
    images = 2
    head_cols = qkv_weight.shape[2]
    head_count = head_cols // HD
    score_scale = 1.0 / math.sqrt(HD)
    cot_all = gather_rows_early(own_cot)
    normed_one, inv_one = layer_norm(own_in)
    normed_all = gather_rows(normed_one.astype(jnp.bfloat16))
    total_rows = normed_all.shape[0]
    block_rows = total_rows // images
    projected = jnp.einsum(
        "td,kdf->ktf", normed_all, qkv_weight, preferred_element_type=jnp.float32
    ).astype(jnp.bfloat16)
    query_heads = projected[0].reshape(images, block_rows, head_count, HD)
    pairs = spread(projected[1:].reshape(2, images, block_rows, head_cols), "seq")
    seq_size = pairs.shape[0]
    length = seq_size * block_rows
    heads = jnp.transpose(pairs, (1, 2, 0, 3, 4)).reshape(2, images, length, head_count, HD)
    key_heads, value_heads = (heads[0], heads[1])
    scores = (
        jnp.einsum("ilhd,imhd->ihlm", query_heads, key_heads, preferred_element_type=jnp.float32)
        * score_scale
    )
    row_max = jnp.max(scores, axis=-1)
    weights = jnp.exp(scores - row_max[..., None])
    totals = jnp.sum(weights, axis=-1)
    log_total = row_max + jnp.log(totals)
    mixed_values = jnp.einsum(
        "ihlm,imhd->ilhd",
        weights.astype(jnp.bfloat16),
        value_heads,
        preferred_element_type=jnp.float32,
    )
    attended = (mixed_values / jnp.transpose(totals, (0, 2, 1))[..., None]).astype(jnp.bfloat16)
    attn_own = scatter_rows(dot_f32(attended.reshape(total_rows, head_cols), out_weight))
    resid = (own_in + attn_own).astype(jnp.bfloat16)
    normed_two, inv_two = layer_norm(resid.astype(jnp.float32))
    normed_two_all = gather_rows(normed_two.astype(jnp.bfloat16))
    hidden_pre = dot_f32(normed_two_all, up_weight)
    hidden = gelu_value(hidden_pre).astype(jnp.bfloat16)
    grad_act = dot_nt(cot_all, down_weight)
    grad_hidden = (grad_act * gelu_slope(hidden_pre)).astype(jnp.bfloat16)
    grad_norm_two = scatter_rows(dot_nt(grad_hidden, up_weight))
    ffn_own = scatter_rows_later(dot_f32(hidden, down_weight))
    block_out = (resid.astype(jnp.float32) + ffn_own).astype(jnp.bfloat16)
    grad_resid = (
        own_cot.astype(jnp.float32) + norm_backward(normed_two, inv_two, grad_norm_two)
    ).astype(jnp.bfloat16)
    grad_resid_all = gather_rows(grad_resid)
    grad_attn = dot_nt(grad_resid_all, out_weight).astype(jnp.bfloat16)
    grad_attn_heads = grad_attn.reshape(images, block_rows, head_count, HD)
    row_delta = jnp.sum(grad_attn_heads.astype(jnp.float32) * attended.astype(jnp.float32), axis=-1)
    prob_rows = jnp.exp(scores - log_total[..., None])
    grad_probs = jnp.einsum(
        "ilhd,imhd->ihlm", grad_attn_heads, value_heads, preferred_element_type=jnp.float32
    )
    grad_scores = (
        prob_rows * (grad_probs - jnp.transpose(row_delta, (0, 2, 1))[..., None]) * score_scale
    ).astype(jnp.bfloat16)
    grad_query = jnp.einsum(
        "ihlm,imhd->ilhd", grad_scores, key_heads, preferred_element_type=jnp.float32
    ).astype(jnp.bfloat16)
    key_terms = jnp.einsum(
        "ihlm,ilhd->imhd", grad_scores, query_heads, preferred_element_type=jnp.float32
    ).astype(jnp.bfloat16)
    value_terms = jnp.einsum(
        "ihlm,ilhd->imhd",
        prob_rows.astype(jnp.bfloat16),
        grad_attn_heads,
        preferred_element_type=jnp.float32,
    ).astype(jnp.bfloat16)
    terms = jnp.stack([key_terms, value_terms]).reshape(2, images, seq_size, block_rows, head_cols)
    terms = lax.all_to_all(jnp.transpose(terms, (2, 0, 1, 3, 4)), "seq", 0, 0)
    grad_kv = jnp.sum(terms.astype(jnp.float32), axis=0).astype(jnp.bfloat16)
    grad_qkv = jnp.concatenate(
        [grad_query.reshape(1, total_rows, head_cols), grad_kv.reshape(2, total_rows, head_cols)]
    )
    grad_norm_one = scatter_rows(
        jnp.einsum("ktf,kdf->td", grad_qkv, qkv_weight, preferred_element_type=jnp.float32)
    )
    grad_input = (
        grad_resid.astype(jnp.float32) + norm_backward(normed_one, inv_one, grad_norm_one)
    ).astype(jnp.bfloat16)
    return (block_out[None], grad_input[None])


def solution(mesh):
    in_specs = (
        P("section", ("seq", "mp"), None),
        P(None, None, ("section", "mp")),
        P(("section", "mp"), None),
        P(None, ("section", "mp")),
        P(("section", "mp"), None),
        P("section", ("seq", "mp"), None),
    )
    out_specs = (P("section", ("seq", "mp"), None), P("section", ("seq", "mp"), None))
    return jax.shard_map(
        per_device, mesh=mesh, in_specs=in_specs, out_specs=out_specs, check_vma=False
    )
```

profile of v0, /device:TPU:0, one launch (start us, length us, event | category | flops | bytes accessed | tf_op | source)
XLA Modules:
  0.0 379.1 jit_solution(5679118020968333429)
XLA Ops:
  7.2 1.2 convert_reduce_fusion.5
  8.4 1.1 fusion.64
  9.5 1.0 fusion.83
  10.6 24.8 %all_to_all.40 = bf16[8,16,4096]{2,1,0:T(8,128)(2,1)S(1)} all-to-all(bf16[8,16,4096]{2,1,0:T(8,128)(2,1)S(1)} %broadcast_in_dim.19), channel_id=1, replica_groups=mesh['section'=2,'seq'=8,'mp'=8] {'mp'}, dimensions={0} | all-to-all | bytes 2097152 | tf_op jit(solution)/shard_map/all_to_all | solution.py:40
  35.4 2.7 collective-permute-done
  38.1 4.6 %fusion.29 = bf16[3,256,256]{2,1,0:T(8,128)(2,1)S(1)} fusion(bf16[3,4096,256]{2,1,0:T(8,128)(2,1)} %param.7, bf16[128,4096]{1,0:T(8,128)(2,1)S(1)} %collective-permute-done, bf16[128,4096]{1,0:T(8,128)(2,1)S(1)} %bitcast.138), kind=kOutput, calls=%fused_computation.48 | convolution fusion | flops 1615003648 | bytes 8781824 | tf_op jit(solution)/shard_map/td,kdf->ktf/dot_general | solution.py:90
  42.9 1.8 broadcast_in_dim.21
  44.7 4.6 %all-to-all-start.1 = ((bf16[8,2,2,128,256]{3,4,2,1,0:T(8,128)(2,1)}), bf16[8,2,2,128,256]{3,4,2,1,0:T(8,128)(2,1)}, u32[]{:S(2)}, u32[]{:S(2)}) async-start(bf16[8,2,2,128,256]{3,4,2,1,0:T(8,128)(2,1)} %broadcast_in_dim.21), calls=%async_computation.1 | async-start | bytes 4194304 | tf_op jit(solution)/shard_map/all_to_all | solution.py:40
  49.5 27.2 %all-to-all-done.1 = bf16[8,2,2,128,256]{3,4,2,1,0:T(8,128)(2,1)} async-done(((bf16[8,2,2,128,256]{3,4,2,1,0:T(8,128)(2,1)}), bf16[8,2,2,128,256]{3,4,2,1,0:T(8,128)(2,1)}, u32[]{:S(2)}, u32[]{:S(2)}) %all-to-all-start.1) | async-done | bytes 2097184 | tf_op jit(solution)/shard_map/all_to_all | solution.py:40
  76.6 2.7 fusion.99
  79.3 1.7 copy.26
  81.0 1.5 squeeze.11
  82.5 3.3 copy.25
  85.8 2.3 squeeze.10
  89.2 0.9 copy-done.1
  90.8 0.7 fusion.85
  91.8 2.6 collective-permute-done.1
  94.6 20.7 %all_to_all.41 = bf16[8,16,4096]{2,1,0:T(8,128)(2,1)S(1)} all-to-all(bf16[8,16,4096]{2,1,0:T(8,128)(2,1)S(1)} %bitcast.130), channel_id=1, replica_groups=mesh['section'=2,'seq'=8,'mp'=8] {'mp'}, dimensions={0} | all-to-all | bytes 2097152 | tf_op jit(solution)/shard_map/all_to_all | solution.py:54
  116.0 1.1 broadcast_in_dim.23
  117.1 4.2 %all-to-all-start.3 = ((bf16[8,16,4096]{2,1,0:T(8,128)(2,1)}), bf16[8,16,4096]{2,1,0:T(8,128)(2,1)}, u32[]{:S(2)}, u32[]{:S(2)}) async-start(bf16[8,16,4096]{2,1,0:T(8,128)(2,1)} %broadcast_in_dim.23), calls=%async_computation.3 | async-start | bytes 2097152 | tf_op jit(solution)/shard_map/all_to_all | solution.py:40
  122.1 13.8 %all-to-all-done.3 = bf16[8,16,4096]{2,1,0:T(8,128)(2,1)} async-done(((bf16[8,16,4096]{2,1,0:T(8,128)(2,1)}), bf16[8,16,4096]{2,1,0:T(8,128)(2,1)}, u32[]{:S(2)}, u32[]{:S(2)}) %all-to-all-start.3) | async-done | bytes 1048608 | tf_op jit(solution)/shard_map/all_to_all | solution.py:40
  135.9 35.0 %all-gather.3.cloned.1.call-done = bf16[1,128,4096]{2,1,0:T(8,128)(2,1)} async-done(((bf16[1,16,4096]{2,1,0:T(8,128)(2,1)}), bf16[1,128,4096]{2,1,0:T(8,128)(2,1)}) %all-gather.3.cloned.1.call-update) | async-done | bytes 1048592 | tf_op jit(solution)/shard_map/all_gather | solution.py:66
  170.9 6.5 %fusion.7 = f32[256,1024]{1,0:T(8,128)S(1)} fusion(bf16[4096,1024]{1,0:T(8,128)(2,1)} %param.9, bf16[128,4096]{1,0:T(8,128)(2,1)} %collective-permute-done.2, bf16[128,4096]{1,0:T(8,128)(2,1)} %bitcast.12), kind=kOutput, calls=%fused_computation.21 | convolution fusion | flops 2151677952 | bytes 11534336 | tf_op jit(solution)/shard_map/dot_general | solution.py:71
  177.5 2.3 fusion.47
  179.9 2.0 copy-done.6
  181.8 1.1 slice.84
  182.9 0.9 collective-permute-start.3
  183.9 13.4 %fusion.45 = f32[256,4096]{1,0:T(8,128)} fusion(bf16[4096,1024]{1,0:T(8,128)(2,1)} %param.9, bf16[1024,4096]{1,0:T(8,128)(2,1)} %param.10, bf16[128,4096]{1,0:T(8,128)(2,1)} %collective-permute-done.4, bf16[128,4096]{1,0:T(8,128)(2,1)} %bitcast.146, f32[256,1024]{1,0:T(8,128)} %copy-done.10), kind=kOutput, calls=%fused_computation.63 | convolution fusion | flops 4301783040 | bytes 24117248 | tf_op jit(solution)/shard_map/tf,df->td/dot_general | solution.py:75
  197.3 2.7 slice.83
  200.0 3.1 fusion.2
  203.1 2.1 fusion.1
  205.2 22.3 %all_to_all.42 = bf16[8,16,4096]{2,1,0:T(8,128)(2,1)S(1)} all-to-all(bf16[8,16,4096]{2,1,0:T(8,128)(2,1)S(1)} %bitcast.131), channel_id=1, replica_groups=mesh['section'=2,'seq'=8,'mp'=8] {'mp'}, dimensions={0} | all-to-all | bytes 2097152 | tf_op jit(solution)/shard_map/all_to_all | solution.py:54
  227.9 48.2 %reduce-scatter.2.cloned.1.call-done = bf16[16,4096]{1,0:T(8,128)(2,1)} async-done(((bf16[128,4096]{1,0:T(8,128)(2,1)}), bf16[16,4096]{1,0:T(8,128)(2,1)}) %reduce-scatter.2.cloned.1.call-update) | async-done | bytes 131088 | tf_op jit(solution)/shard_map/reduce_scatter | solution.py:62
  276.1 1.7 fusion.63
  278.1 19.8 %all_to_all.43 = bf16[8,16,4096]{2,1,0:T(8,128)(2,1)S(1)} all-to-all(bf16[8,16,4096]{2,1,0:T(8,128)(2,1)S(1)} %broadcast_in_dim.26), channel_id=1, replica_groups=mesh['section'=2,'seq'=8,'mp'=8] {'mp'}, dimensions={0} | all-to-all | bytes 2097152 | tf_op jit(solution)/shard_map/all_to_all | solution.py:40
  297.9 2.6 collective-permute-done.6
  300.5 0.7 fusion.32
  301.5 2.3 convolution_convert_fusion
  303.8 2.0 multiply_convert_fusion
  307.2 1.5 maximum_bitcast_fusion.2
  308.7 4.3 %all-to-all-start.6 = ((bf16[8,2,2,128,256]{3,4,2,1,0:T(8,128)(2,1)}), bf16[8,2,2,128,256]{3,4,2,1,0:T(8,128)(2,1)}, u32[]{:S(2)}, u32[]{:S(2)}) async-start(bf16[8,2,2,128,256]{3,4,2,1,0:T(8,128)(2,1)} %maximum_bitcast_fusion.2), calls=%async_computation.7 | async-start | bytes 4194304 | tf_op jit(solution)/shard_map/all_to_all | solution.py:152
  313.1 1.7 fusion.35
  315.0 25.7 %all-to-all-done.6 = bf16[8,2,2,128,256]{3,4,2,1,0:T(8,128)(2,1)} async-done(((bf16[8,2,2,128,256]{3,4,2,1,0:T(8,128)(2,1)}), bf16[8,2,2,128,256]{3,4,2,1,0:T(8,128)(2,1)}, u32[]{:S(2)}, u32[]{:S(2)}) %all-to-all-start.6) | async-done | bytes 2097184 | tf_op jit(solution)/shard_map/all_to_all | solution.py:152
  340.6 1.9 reduce_sum.147
  342.7 4.6 %convolution_bitcast_fusion = f32[256,4096]{1,0:T(8,128)S(1)} fusion(bf16[3,4096,256]{2,1,0:T(8,128)(2,1)} %param.7, bf16[2,256,256]{2,1,0:T(8,128)(2,1)S(1)} %bitcast.134, bf16[1,256,256]{2,1,0:T(8,128)(2,1)S(1)} %reshape.277), kind=kOutput, calls=%fused_computation | convolution fusion | flops 1610809344 | bytes 10878976 | tf_op jit(solution)/shard_map/ktf,kdf->td/dot_general | solution.py:158
  347.6 2.6 collective-permute-done.7
  350.4 20.3 %all_to_all.44 = bf16[8,16,4096]{2,1,0:T(8,128)(2,1)S(1)} all-to-all(bf16[8,16,4096]{2,1,0:T(8,128)(2,1)S(1)} %bitcast.132), channel_id=1, replica_groups=mesh['section'=2,'seq'=8,'mp'=8] {'mp'}, dimensions={0} | all-to-all | bytes 2097152 | tf_op jit(solution)/shard_map/all_to_all | solution.py:54
  371.4 0.8 fusion.75
  (82 shorter events, 8.0 us)
Async XLA Ops:
  7.2 83.7 %copy-start = (bf16[256,4096]{1,0:T(8,128)(2,1)S(1)}, bf16[256,4096]{1,0:T(8,128)(2,1)}, u32[]{:S(2)}) copy-start(bf16[256,4096]{1,0:T(8,128)(2,1)} %param.8) | copy-start | bytes 6291460
  35.4 2.7 collective-permute-start
  44.7 32.0 %all-to-all-start.1 = ((bf16[8,2,2,128,256]{3,4,2,1,0:T(8,128)(2,1)}), bf16[8,2,2,128,256]{3,4,2,1,0:T(8,128)(2,1)}, u32[]{:S(2)}, u32[]{:S(2)}) async-start(bf16[8,2,2,128,256]{3,4,2,1,0:T(8,128)(2,1)} %broadcast_in_dim.21), calls=%async_computation.1 | async-start | bytes 4194304 | tf_op jit(solution)/shard_map/all_to_all | solution.py:40
  49.4 38.7 %copy-start.7 = (bf16[2,128,2,128]{1,3,2,0:T(8,128)(2,1)}, bf16[2,128,2,128]{1,3,2,0:T(8,128)(2,1)S(1)}, u32[]{:S(2)}) copy-start(bf16[2,128,2,128]{1,3,2,0:T(8,128)(2,1)S(1)} %copy.34) | copy-start | bytes 393220
  82.5 5.6 %copy-start.3 = (bf16[2,1024,2,128]{1,3,2,0:T(8,128)(2,1)}, bf16[2,1024,2,128]{1,3,2,0:T(8,128)(2,1)S(1)}, u32[]{:S(2)}) copy-start(bf16[2,1024,2,128]{1,3,2,0:T(8,128)(2,1)S(1)} %squeeze.11) | copy-start | bytes 3145732
  88.1 2.0 copy-start.5
  88.7 1.4 copy-start.1
  91.7 2.7 collective-permute-start.1
  94.6 20.8 %copy-start.4 = (bf16[1,16,4096]{2,1,0:T(8,128)(2,1)S(1)}, bf16[1,16,4096]{2,1,0:T(8,128)(2,1)}, u32[]{:S(2)}) copy-start(bf16[1,16,4096]{2,1,0:T(8,128)(2,1)} %param.6) | copy-start | bytes 393220
  117.1 18.8 %all-to-all-start.3 = ((bf16[8,16,4096]{2,1,0:T(8,128)(2,1)}), bf16[8,16,4096]{2,1,0:T(8,128)(2,1)}, u32[]{:S(2)}, u32[]{:S(2)}) async-start(bf16[8,16,4096]{2,1,0:T(8,128)(2,1)} %broadcast_in_dim.23), calls=%async_computation.3 | async-start | bytes 2097152 | tf_op jit(solution)/shard_map/all_to_all | solution.py:40
  121.3 49.6 %all-gather.3.cloned.1.call-start = ((), (), s32[]{:S(2)}) async-start(), calls=%async_computation.10 | async-start | bytes 1179648 | tf_op jit(solution)/shard_map/all_gather | solution.py:66
  122.1 154.0 %reduce-scatter.2.cloned.1.call-start = ((), (), s32[]{:S(2)}) async-start(), calls=%async_computation.9 | async-start | bytes 1179648 | tf_op jit(solution)/shard_map/reduce_scatter | solution.py:62
  135.9 35.1 %collective-permute-start.2 = (bf16[128,4096]{1,0:T(8,128)(2,1)}, bf16[128,4096]{1,0:T(8,128)(2,1)}, u32[]{:S(2)}, u32[]{:S(2)}) collective-permute-start(bf16[128,4096]{1,0:T(8,128)(2,1)} %bitcast.12), channel_id=1, source_target_pairs={{0,64},{64,0},{1,65},{65,1},{2,66},{66,2},{3,67},{67,3},{4,68},{68... | collective-permute-start | bytes 3145736 | tf_op jit(solution)/shard_map/ppermute | solution.py:34
  170.9 6.5 %slice-start = ((s8[8388608]{0:T(1024)(128)(4,1)}), s8[4194304]{0:T(1024)(128)(4,1)S(1)}, s32[]{:S(2)}) async-start(s8[8388608]{0:T(1024)(128)(4,1)} %bitcast.143), calls=%async_computation.11 | async-start | bytes 8388608
  170.9 6.5 %slice-start.1 = ((s8[8388608]{0:T(1024)(128)(4,1)}), s8[4194304]{0:T(1024)(128)(4,1)S(1)}, s32[]{:S(2)}) async-start(s8[8388608]{0:T(1024)(128)(4,1)} %bitcast.143), calls=%async_computation.12 | async-start | bytes 8388608
  170.9 12.9 %collective-permute-start.4 = (bf16[128,4096]{1,0:T(8,128)(2,1)}, bf16[128,4096]{1,0:T(8,128)(2,1)}, u32[]{:S(2)}, u32[]{:S(2)}) collective-permute-start(bf16[128,4096]{1,0:T(8,128)(2,1)} %bitcast.145), channel_id=1, source_target_pairs={{0,64},{64,0},{1,65},{65,1},{2,66},{66,2},{3,67},{67,3},{4,68},{68... | collective-permute-start | bytes 3145736 | tf_op jit(solution)/shard_map/ppermute | solution.py:34
  177.5 2.4 copy-start.10
  179.8 2.0 copy-start.6
  182.9 17.1 %collective-permute-start.3 = (bf16[128,4096]{1,0:T(8,128)(2,1)}, bf16[128,4096]{1,0:T(8,128)(2,1)}, u32[]{:S(2)}, u32[]{:S(2)}) collective-permute-start(bf16[128,4096]{1,0:T(8,128)(2,1)} %slice.84), channel_id=1, source_target_pairs={{0,64},{64,0},{1,65},{65,1},{2,66},{66,2},{3,67},{67,3},{4,68},{68... | collective-permute-start | bytes 3145736 | tf_op jit(solution)/shard_map/ppermute | solution.py:34
  200.0 3.1 collective-permute-start.5
  205.2 72.7 %copy-start.9 = (bf16[1,16,4096]{2,1,0:T(8,128)(2,1)S(1)}, bf16[1,16,4096]{2,1,0:T(8,128)(2,1)}, u32[]{:S(2)}) copy-start(bf16[1,16,4096]{2,1,0:T(8,128)(2,1)} %param.11) | copy-start | bytes 393220
  297.9 2.7 collective-permute-start.6
  301.4 2.3 copy-start.2
  303.8 2.0 copy-start.8
  308.7 31.9 %all-to-all-start.6 = ((bf16[8,2,2,128,256]{3,4,2,1,0:T(8,128)(2,1)}), bf16[8,2,2,128,256]{3,4,2,1,0:T(8,128)(2,1)}, u32[]{:S(2)}, u32[]{:S(2)}) async-start(bf16[8,2,2,128,256]{3,4,2,1,0:T(8,128)(2,1)} %maximum_bitcast_fusion.2), calls=%async_computation.7 | async-start | bytes 4194304 | tf_op jit(solution)/shard_map/all_to_all | solution.py:152
  347.5 2.7 collective-permute-start.7
Sparse Core Ops, SparseCore 0:
  124.5 46.3 all-gather.2
  203.2 72.8 reduce-scatter.1
where the time goes:
time: 380 us; the launch traced here: 379 us
  waiting for transfers between devices  161 us (42%)
  blocking collectives  108 us (28%)
  matrix products  40.4 us (11%)
  local copies, waits for them, and re-layouts  23.5 us (6%)
  other arithmetic  17.3 us (5%)
  between operations  14.5 us (4%)
  starting transfers between devices  14.4 us (4%)
    all_to_all x3, blocking collectives, scatter_rows(): parts = lax.all_to_all(pair.reshape(size, half // size, width), 'mp', 0, 0)  63.3 us
    reduce_scatter x1, waiting for transfers between devices, scatter_rows_later(): lax.psum_scatter(pair, 'mp', scatter_dimension=0, tiled=True)  48.2 us
    all_to_all x2, blocking collectives, spread(): return lax.all_to_all(copies, axis, 0, 0)  44.6 us
    all_to_all x2, waiting for transfers between devices, spread(): return lax.all_to_all(copies, axis, 0, 0)  41 us
    all_gather x1, waiting for transfers between devices, gather_rows_early(): mine = lax.all_gather(own, 'mp', axis=0, tiled=True)  35 us
    all_to_all x1, waiting for transfers between devices, per_device(): terms = lax.all_to_all(jnp.transpose(terms, (2, 0, 1, 3, 4)), 'seq', 0, 0)  25.7 us
    dot_general x2, matrix products, dot_nt(): return jnp.einsum('tf,df->td', lhs, rhs, preferred_element_type=jnp.float32)  14.2 us
    ppermute x8, waiting for transfers between devices, swap_section(): return lax.ppermute(data, 'section', [(0, 1), (1, 0)])  10.6 us
  transfers between devices with their start and end apart: 13, of which 9 were waited for; matrix products, arithmetic and copies ran while one was open for 9% of the time, Pallas kernels for 0%

commit v1 on v0

--- a/solution.py
+++ b/solution.py
@@ -63,7 +63,15 @@
 
 
 def gather_rows_early(own):
-    mine = lax.all_gather(own, "mp", axis=0, tiled=True)
+    mine = jnp.concatenate(
+        lax.all_to_all(
+            jnp.stack([own for _ in range(lax.axis_size("mp"))], axis=0),
+            axis_name="mp",
+            split_axis=0,
+            concat_axis=0,
+        ),
+        axis=0,
+    )
     return jnp.concatenate([mine, swap_section(mine)], axis=0)
 
 

time: 380 us -> 362 us (0.953)
  waiting for transfers between devices: 161 us -> 110 us
  blocking collectives: 108 us -> 146 us
  starting transfers between devices: 14.4 us -> 9.97 us
    all_gather x1 -> x0, waiting for transfers between devices: 35 us -> none  [gather_rows_early(): mine = lax.all_gather(own, 'mp', axis=0, tiled=True)]
    all_to_all x0 -> x1, blocking collectives: none -> 20.3 us  [gather_rows_early(): lax.all_to_all(jnp.stack([own for _ in range(lax.axis_size('mp'))], axis=...]
    all_to_all x2 -> x3, blocking collectives: 44.6 us -> 63.9 us  [spread(): return lax.all_to_all(copies, axis, 0, 0)]
    all_to_all x2 -> x1, waiting for transfers between devices: 41 us -> 27.1 us  [spread(): return lax.all_to_all(copies, axis, 0, 0)]
    all_to_all x2 -> x1, starting transfers between devices: 8.84 us -> 4.59 us  [spread(): return lax.all_to_all(copies, axis, 0, 0)]
  transfers between devices with their start and end apart: 13 -> 11, of which waited for: 9 -> 7; matrix products, arithmetic and copies ran while one was open for 9% -> 9% of each run, Pallas kernels for 0% -> 0%
where the time goes in v1:
time: 362 us; the launch traced here: 361 us
  blocking collectives  146 us (40%)
  waiting for transfers between devices  110 us (30%)
  matrix products  40 us (11%)
  local copies, waits for them, and re-layouts  22.6 us (6%)
  other arithmetic  17.3 us (5%)
  between operations  14.5 us (4%)
  starting transfers between devices  9.97 us (3%)
    all_to_all x3, blocking collectives, spread(): return lax.all_to_all(copies, axis, 0, 0)  63.9 us
    all_to_all x3, blocking collectives, scatter_rows(): parts = lax.all_to_all(pair.reshape(size, half // size, width), 'mp', 0, 0)  62.1 us
    reduce_scatter x1, waiting for transfers between devices, scatter_rows_later(): lax.psum_scatter(pair, 'mp', scatter_dimension=0, tiled=True)  47 us
    all_to_all x1, waiting for transfers between devices, spread(): return lax.all_to_all(copies, axis, 0, 0)  27.1 us
    all_to_all x1, waiting for transfers between devices, per_device(): terms = lax.all_to_all(jnp.transpose(terms, (2, 0, 1, 3, 4)), 'seq', 0, 0)  25.7 us
    all_to_all x1, blocking collectives, gather_rows_early(): lax.all_to_all(jnp.stack([own for _ in range(lax.axis_size('mp'))], axis=...  20.3 us
    dot_general x2, matrix products, dot_nt(): return jnp.einsum('tf,df->td', lhs, rhs, preferred_element_type=jnp.float32)  14.2 us
    ppermute x8, waiting for transfers between devices, swap_section(): return lax.ppermute(data, 'section', [(0, 1), (1, 0)])  10.6 us
  transfers between devices with their start and end apart: 11, of which 7 were waited for; matrix products, arithmetic and copies ran while one was open for 9% of the time, Pallas kernels for 0%

profile of v1, /device:TPU:0, one launch (start us, length us, event | category | flops | bytes accessed | tf_op | source)
XLA Modules:
  0.0 361.2 jit_solution(333533420874266894)
XLA Ops:
  7.2 1.2 convert_reduce_fusion.5
  8.4 1.1 fusion.64
  9.5 1.0 fusion.83
  10.6 24.8 %all_to_all.45 = bf16[8,16,4096]{2,1,0:T(8,128)(2,1)S(1)} all-to-all(bf16[8,16,4096]{2,1,0:T(8,128)(2,1)S(1)} %broadcast_in_dim.19), channel_id=1, replica_groups=mesh['section'=2,'seq'=8,'mp'=8] {'mp'}, dimensions={0} | all-to-all | bytes 2097152 | tf_op jit(solution)/shard_map/all_to_all | solution.py:40
  35.4 2.7 collective-permute-done
  38.1 4.6 %fusion.29 = bf16[3,256,256]{2,1,0:T(8,128)(2,1)S(1)} fusion(bf16[3,4096,256]{2,1,0:T(8,128)(2,1)} %param.7, bf16[128,4096]{1,0:T(8,128)(2,1)S(1)} %collective-permute-done, bf16[128,4096]{1,0:T(8,128)(2,1)S(1)} %bitcast.143), kind=kOutput, calls=%fused_computation.48 | convolution fusion | flops 1615003648 | bytes 8781824 | tf_op jit(solution)/shard_map/td,kdf->ktf/dot_general | solution.py:98
  42.9 1.8 broadcast_in_dim.21
  44.7 4.6 %all-to-all-start.1 = ((bf16[8,2,2,128,256]{3,4,2,1,0:T(8,128)(2,1)}), bf16[8,2,2,128,256]{3,4,2,1,0:T(8,128)(2,1)}, u32[]{:S(2)}, u32[]{:S(2)}) async-start(bf16[8,2,2,128,256]{3,4,2,1,0:T(8,128)(2,1)} %broadcast_in_dim.21), calls=%async_computation.1 | async-start | bytes 4194304 | tf_op jit(solution)/shard_map/all_to_all | solution.py:40
  49.5 27.1 %all-to-all-done.1 = bf16[8,2,2,128,256]{3,4,2,1,0:T(8,128)(2,1)} async-done(((bf16[8,2,2,128,256]{3,4,2,1,0:T(8,128)(2,1)}), bf16[8,2,2,128,256]{3,4,2,1,0:T(8,128)(2,1)}, u32[]{:S(2)}, u32[]{:S(2)}) %all-to-all-start.1) | async-done | bytes 2097184 | tf_op jit(solution)/shard_map/all_to_all | solution.py:40
  76.6 2.7 fusion.99
  79.3 1.7 copy.26
  81.0 1.5 squeeze.9
  82.5 3.3 copy.25
  85.8 2.3 squeeze.8
  88.1 0.6 fusion.100
  89.2 0.9 copy-done.1
  90.1 0.6 fusion.31
  90.8 0.7 fusion.85
  91.8 2.6 collective-permute-done.1
  94.6 20.7 %all_to_all.46 = bf16[8,16,4096]{2,1,0:T(8,128)(2,1)S(1)} all-to-all(bf16[8,16,4096]{2,1,0:T(8,128)(2,1)S(1)} %bitcast.131), channel_id=1, replica_groups=mesh['section'=2,'seq'=8,'mp'=8] {'mp'}, dimensions={0} | all-to-all | bytes 2097152 | tf_op jit(solution)/shard_map/all_to_all | solution.py:54
  116.1 19.3 %all_to_all.47 = bf16[8,16,4096]{2,1,0:T(8,128)(2,1)S(1)} all-to-all(bf16[8,16,4096]{2,1,0:T(8,128)(2,1)S(1)} %broadcast_in_dim.23), channel_id=1, replica_groups=mesh['section'=2,'seq'=8,'mp'=8] {'mp'}, dimensions={0} | all-to-all | bytes 2097152 | tf_op jit(solution)/shard_map/all_to_all | solution.py:40
  135.5 20.3 %all_to_all.48 = bf16[8,16,4096]{2,1,0:T(8,128)(2,1)S(1)} all-to-all(bf16[8,16,4096]{2,1,0:T(8,128)(2,1)S(1)} %stack.12), channel_id=1, replica_groups=mesh['section'=2,'seq'=8,'mp'=8] {'mp'}, dimensions={0} | all-to-all | bytes 2097152 | tf_op jit(solution)/shard_map/all_to_all | solution.py:67
  155.8 6.1 %fusion.7 = f32[256,1024]{1,0:T(8,128)S(1)} fusion(bf16[4096,1024]{1,0:T(8,128)(2,1)} %param.9, bf16[128,4096]{1,0:T(8,128)(2,1)S(1)} %collective-permute-done.2, bf16[128,4096]{1,0:T(8,128)(2,1)S(1)} %bitcast.139), kind=kOutput, calls=%fused_computation.21 | convolution fusion | flops 2151677952 | bytes 11534336 | tf_op jit(solution)/shard_map/dot_general | solution.py:79
  162.0 2.3 fusion.47
  164.3 2.0 copy-done.6
  166.3 1.1 slice.84
  167.4 0.8 collective-permute-start.3
  168.2 13.4 %fusion.45 = f32[256,4096]{1,0:T(8,128)} fusion(bf16[4096,1024]{1,0:T(8,128)(2,1)} %param.9, bf16[1024,4096]{1,0:T(8,128)(2,1)} %param.10, bf16[128,4096]{1,0:T(8,128)(2,1)} %collective-permute-done.4, bf16[128,4096]{1,0:T(8,128)(2,1)} %bitcast.137, f32[256,1024]{1,0:T(8,128)} %copy-done.11), kind=kOutput, calls=%fused_computation.63 | convolution fusion | flops 4301783040 | bytes 24117248 | tf_op jit(solution)/shard_map/tf,df->td/dot_general | solution.py:83
  181.7 2.7 slice.83
  184.4 3.0 fusion.2
  187.5 2.1 fusion.1
  189.5 21.1 %all_to_all.49 = bf16[8,16,4096]{2,1,0:T(8,128)(2,1)S(1)} all-to-all(bf16[8,16,4096]{2,1,0:T(8,128)(2,1)S(1)} %bitcast.132), channel_id=1, replica_groups=mesh['section'=2,'seq'=8,'mp'=8] {'mp'}, dimensions={0} | all-to-all | bytes 2097152 | tf_op jit(solution)/shard_map/all_to_all | solution.py:54
  211.1 47.0 %reduce-scatter.2.cloned.1.call-done = bf16[16,4096]{1,0:T(8,128)(2,1)} async-done(((bf16[128,4096]{1,0:T(8,128)(2,1)}), bf16[16,4096]{1,0:T(8,128)(2,1)}) %reduce-scatter.2.cloned.1.call-update) | async-done | bytes 131088 | tf_op jit(solution)/shard_map/reduce_scatter | solution.py:62
  258.2 1.7 fusion.63
  260.1 19.8 %all_to_all.50 = bf16[8,16,4096]{2,1,0:T(8,128)(2,1)S(1)} all-to-all(bf16[8,16,4096]{2,1,0:T(8,128)(2,1)S(1)} %broadcast_in_dim.26), channel_id=1, replica_groups=mesh['section'=2,'seq'=8,'mp'=8] {'mp'}, dimensions={0} | all-to-all | bytes 2097152 | tf_op jit(solution)/shard_map/all_to_all | solution.py:40
  280.0 2.6 collective-permute-done.6
  282.6 0.7 fusion.32
  283.6 2.3 convolution_convert_fusion
  285.9 2.0 multiply_convert_fusion
  289.3 1.5 maximum_bitcast_fusion.2
  290.8 4.3 %all-to-all-start.7 = ((bf16[8,2,2,128,256]{3,4,2,1,0:T(8,128)(2,1)}), bf16[8,2,2,128,256]{3,4,2,1,0:T(8,128)(2,1)}, u32[]{:S(2)}, u32[]{:S(2)}) async-start(bf16[8,2,2,128,256]{3,4,2,1,0:T(8,128)(2,1)} %maximum_bitcast_fusion.2), calls=%async_computation.8 | async-start | bytes 4194304 | tf_op jit(solution)/shard_map/all_to_all | solution.py:160
  295.1 1.7 fusion.35
  297.0 25.7 %all-to-all-done.7 = bf16[8,2,2,128,256]{3,4,2,1,0:T(8,128)(2,1)} async-done(((bf16[8,2,2,128,256]{3,4,2,1,0:T(8,128)(2,1)}), bf16[8,2,2,128,256]{3,4,2,1,0:T(8,128)(2,1)}, u32[]{:S(2)}, u32[]{:S(2)}) %all-to-all-start.7) | async-done | bytes 2097184 | tf_op jit(solution)/shard_map/all_to_all | solution.py:160
  322.7 1.9 reduce_sum.147
  324.8 4.6 %convolution_bitcast_fusion = f32[256,4096]{1,0:T(8,128)S(1)} fusion(bf16[3,4096,256]{2,1,0:T(8,128)(2,1)} %param.7, bf16[2,256,256]{2,1,0:T(8,128)(2,1)S(1)} %bitcast.135, bf16[1,256,256]{2,1,0:T(8,128)(2,1)S(1)} %reshape.282), kind=kOutput, calls=%fused_computation | convolution fusion | flops 1610809344 | bytes 10878976 | tf_op jit(solution)/shard_map/ktf,kdf->td/dot_general | solution.py:166
  329.6 2.6 collective-permute-done.7
  332.5 20.3 %all_to_all.51 = bf16[8,16,4096]{2,1,0:T(8,128)(2,1)S(1)} all-to-all(bf16[8,16,4096]{2,1,0:T(8,128)(2,1)S(1)} %bitcast.133), channel_id=1, replica_groups=mesh['section'=2,'seq'=8,'mp'=8] {'mp'}, dimensions={0} | all-to-all | bytes 2097152 | tf_op jit(solution)/shard_map/all_to_all | solution.py:54
  353.5 0.8 fusion.75
  (82 shorter events, 6.3 us)
Async XLA Ops:
  7.2 83.7 %copy-start = (bf16[256,4096]{1,0:T(8,128)(2,1)S(1)}, bf16[256,4096]{1,0:T(8,128)(2,1)}, u32[]{:S(2)}) copy-start(bf16[256,4096]{1,0:T(8,128)(2,1)} %param.8) | copy-start | bytes 6291460
  35.4 2.7 collective-permute-start
  44.7 32.0 %all-to-all-start.1 = ((bf16[8,2,2,128,256]{3,4,2,1,0:T(8,128)(2,1)}), bf16[8,2,2,128,256]{3,4,2,1,0:T(8,128)(2,1)}, u32[]{:S(2)}, u32[]{:S(2)}) async-start(bf16[8,2,2,128,256]{3,4,2,1,0:T(8,128)(2,1)} %broadcast_in_dim.21), calls=%async_computation.1 | async-start | bytes 4194304 | tf_op jit(solution)/shard_map/all_to_all | solution.py:40
  49.3 208.9 %reduce-scatter.2.cloned.1.call-start = ((), (), s32[]{:S(2)}) async-start(), calls=%async_computation.10 | async-start | bytes 1179648 | tf_op jit(solution)/shard_map/reduce_scatter | solution.py:62
  49.5 38.6 %copy-start.7 = (bf16[2,128,2,128]{1,3,2,0:T(8,128)(2,1)}, bf16[2,128,2,128]{1,3,2,0:T(8,128)(2,1)S(1)}, u32[]{:S(2)}) copy-start(bf16[2,128,2,128]{1,3,2,0:T(8,128)(2,1)S(1)} %copy.34) | copy-start | bytes 393220
  82.5 5.6 %copy-start.3 = (bf16[2,1024,2,128]{1,3,2,0:T(8,128)(2,1)}, bf16[2,1024,2,128]{1,3,2,0:T(8,128)(2,1)S(1)}, u32[]{:S(2)}) copy-start(bf16[2,1024,2,128]{1,3,2,0:T(8,128)(2,1)S(1)} %squeeze.9) | copy-start | bytes 3145732
  88.1 2.0 copy-start.5
  88.7 1.4 copy-start.1
  91.7 2.7 collective-permute-start.1
  94.6 20.8 %copy-start.4 = (bf16[1,16,4096]{2,1,0:T(8,128)(2,1)S(1)}, bf16[1,16,4096]{2,1,0:T(8,128)(2,1)}, u32[]{:S(2)}) copy-start(bf16[1,16,4096]{2,1,0:T(8,128)(2,1)} %param.6) | copy-start | bytes 393220
  115.6 19.8 %copy-start.10 = (bf16[1,16,4096]{2,1,0:T(8,128)(2,1)S(1)}, bf16[1,16,4096]{2,1,0:T(8,128)(2,1)}, u32[]{:S(2)}) copy-start(bf16[1,16,4096]{2,1,0:T(8,128)(2,1)} %param.11) | copy-start | bytes 393220
  135.4 20.4 %collective-permute-start.2 = (bf16[128,4096]{1,0:T(8,128)(2,1)S(1)}, bf16[128,4096]{1,0:T(8,128)(2,1)S(1)}, u32[]{:S(2)}, u32[]{:S(2)}) collective-permute-start(bf16[128,4096]{1,0:T(8,128)(2,1)S(1)} %bitcast.138), channel_id=1, source_target_pairs={{0,64},{64,0},{1,65},{65,1},{2,66},{66,2},{3,67},{67,3},{4,68},{68... | collective-permute-start | bytes 3145736 | tf_op jit(solution)/shard_map/ppermute | solution.py:34
  155.8 6.2 %copy-start.9 = (bf16[8,16,4096]{2,1,0:T(8,128)(2,1)}, bf16[8,16,4096]{2,1,0:T(8,128)(2,1)S(1)}, u32[]{:S(2)}) copy-start(bf16[8,16,4096]{2,1,0:T(8,128)(2,1)S(1)} %all_to_all.48) | copy-start | bytes 3145732
  155.8 6.2 %slice-start = ((s8[8388608]{0:T(1024)(128)(4,1)}), s8[4194304]{0:T(1024)(128)(4,1)S(1)}, s32[]{:S(2)}) async-start(s8[8388608]{0:T(1024)(128)(4,1)} %bitcast.149), calls=%async_computation.11 | async-start | bytes 8388608
  155.8 6.2 %slice-start.1 = ((s8[8388608]{0:T(1024)(128)(4,1)}), s8[4194304]{0:T(1024)(128)(4,1)S(1)}, s32[]{:S(2)}) async-start(s8[8388608]{0:T(1024)(128)(4,1)} %bitcast.149), calls=%async_computation.12 | async-start | bytes 8388608
  155.8 12.5 %collective-permute-start.4 = (bf16[128,4096]{1,0:T(8,128)(2,1)S(1)}, bf16[128,4096]{1,0:T(8,128)(2,1)}, u32[]{:S(2)}, u32[]{:S(2)}) collective-permute-start(bf16[128,4096]{1,0:T(8,128)(2,1)S(1)} %bitcast.136), channel_id=1, source_target_pairs={{0,64},{64,0},{1,65},{65,1},{2,66},{66,2},{3,67},{67,3},{4,68},{68... | collective-permute-start | bytes 3145736 | tf_op jit(solution)/shard_map/ppermute | solution.py:34
  162.0 2.3 copy-start.11
  164.3 2.0 copy-start.6
  167.4 17.0 %collective-permute-start.3 = (bf16[128,4096]{1,0:T(8,128)(2,1)}, bf16[128,4096]{1,0:T(8,128)(2,1)}, u32[]{:S(2)}, u32[]{:S(2)}) collective-permute-start(bf16[128,4096]{1,0:T(8,128)(2,1)} %slice.84), channel_id=1, source_target_pairs={{0,64},{64,0},{1,65},{65,1},{2,66},{66,2},{3,67},{67,3},{4,68},{68... | collective-permute-start | bytes 3145736 | tf_op jit(solution)/shard_map/ppermute | solution.py:34
  184.4 3.1 collective-permute-start.5
  280.0 2.7 collective-permute-start.6
  283.5 2.3 copy-start.2
  285.9 2.0 copy-start.8
  290.8 31.9 %all-to-all-start.7 = ((bf16[8,2,2,128,256]{3,4,2,1,0:T(8,128)(2,1)}), bf16[8,2,2,128,256]{3,4,2,1,0:T(8,128)(2,1)}, u32[]{:S(2)}, u32[]{:S(2)}) async-start(bf16[8,2,2,128,256]{3,4,2,1,0:T(8,128)(2,1)} %maximum_bitcast_fusion.2), calls=%async_computation.8 | async-start | bytes 4194304 | tf_op jit(solution)/shard_map/all_to_all | solution.py:160
  329.5 2.7 collective-permute-start.7
Sparse Core Ops, SparseCore 0:
  187.6 70.5 reduce-scatter.1
